TPU v7x, 32 devices: a whole 2x2x4 slice. The times are simulated.
32 devices in a mesh: dp: 32 (over z, y, x, core).
Axes of the slice: x: 2, y: 2, z: 4, core: 2. Of those that a mesh axis runs over, the one named last changes fastest.
Arguments:
- actions: float32 [16384, 256], P('dp'), may hold values from -6 to 6
- observed: bfloat16 [1024, 196, 256], P('dp'), may hold values from -6 to 6
- camera_flags: int32 [1024], P('dp'), may hold values 0 or 1
- noise_levels: int32 [1024], P('dp'), may hold values from 0 to 99
- cotangent: float32 [16384, 256], P('dp'), may hold values from -6 to 6
- square_weights: float32 [5, 256, 256], P(None, 'dp'), may hold values from -2 to 2
- mlp_weights: float32 [2, 256, 1024], P(None, 'dp'), may hold values from -0.25 to 0.25
- gains: float32 [2, 256], P(None, 'dp'), may hold values from 0.5 to 1.5
- square_moment: float32 [5, 256, 256], P(None, 'dp'), may hold values from -563.2 to 563.2
- mlp_moment: float32 [2, 256, 1024], P(None, 'dp'), may hold values from -307.2 to 307.2
- gain_moment: float32 [2, 256], P(None, 'dp'), may hold values from -640 to 640
Outputs:
- output: float32 [16384, 256], P('dp')
- actions_grad: float32 [16384, 256], P('dp')
- observed_grad: float32 [1024, 196, 256], P('dp')
- square_grad: float32 [5, 256, 256], P(None, 'dp')
- square_moment_new: float32 [5, 256, 256], P(None, 'dp')
- updated_square_projections: float32 [5, 256, 256], P(None, 'dp')
- square_copy: bfloat16 [5, 256, 256], P(None, 'dp')
- mlp_grad: float32 [2, 256, 1024], P(None, 'dp')
- mlp_moment_new: float32 [2, 256, 1024], P(None, 'dp')
- mlp_new: float32 [2, 256, 1024], P(None, 'dp')
- mlp_copy: bfloat16 [2, 256, 1024], P(None, 'dp')
- gain_grad: float32 [2, 256], P(None, 'dp')
- gain_moment_new: float32 [2, 256], P(None, 'dp')
- gains_new: float32 [2, 256], P(None, 'dp')
All inputs are finite; a program needn't handle non-finite values. No bound on the sum of `camera_flags` on one device may be relied on, other than what follows from the above.
Results may differ from a plain program's by a relative error of at most 0.013.
Values may be sent and summed in bfloat16 or wider, within the bound.
A program may use at most 128 MiB of HBM per device.

v0:
```python
import functools
import math

import jax
import jax.numpy as jnp
from jax import lax
from jax.experimental import pallas as pl
from jax.experimental.pallas import tpu as pltpu
from jax.sharding import PartitionSpec as P

HEADS = 4
ACT = 16
OBS_FULL = 196
OBS_FEW = 49
COEF_A = 3.4445
COEF_B = -4.775
COEF_C = 2.0315
F32 = jnp.float32
BF16 = jnp.bfloat16
MESH = pl.DeviceIdType.MESH
VMEM = pltpu.VMEM
NN = (((1,), (0,)), ((), ()))
NT = (((1,), (1,)), ((), ()))
TN = (((0,), (0,)), ((), ()))

LANES = 128
TILE = 8
MLP_ROWS = 64
SQ_ROWS = 16
SQ_AT = (160, 192, 176, 128, 144)
GAIN_BASE = 208
WIRE = 224
PIECES = ((0, 32), (32, 32), (64, 32), (96, 32), (128, 32), (160, 32), (192, 32))
PIECE_X_FIRST = (True, False, True, False, True, True, False)
CHUNKS = ((0, 32), (32, 32), (64, 32), (96, 32), (128, 32), (160, 32), (192, 16), (208, 16))
X_FIRST = (True, False, True, False, True, False, True, False)
PARTS_OUT = (
    (0, 0, 0, 32, 0),
    (1, 0, 32, 32, 32),
    (2, 1, 64, 32, 0),
    (3, 1, 96, 32, 32),
    (4, 5, 128, 16, 0),
    (4, 6, 144, 16, 0),
    (5, 2, 160, 16, 0),
    (5, 4, 176, 16, 0),
    (6, 3, 192, 16, 0),
)
MLP_RATES = (1.0, 0.5)
SQ_RATES = (0.5, 0.5, 0.5, 0.5, 4.0)
GRID = (4, 2, 2, 2)
OWNERS = (8, 22, 14, 16, 11, 21, 13)
SHIFTS = (0.0, 0.0, 0.4, 0.8, 0.8)
KEYS_PAD = 208
GROUP = 16
ROWS = 512


class Refs:
    def __init__(self, pairs):
        self.__dict__.update(pairs)


def dot(left, right, dims=NN):
    return lax.dot_general(left, right, dims, preferred_element_type=F32)


def place():
    me = lax.axis_index("dp")
    return me, me // 8, (me // 4) % 2, (me // 2) % 2, me % 2


def device_at(z, y, x, c):
    return ((z * 2 + y) * 2 + x) * 2 + c


def link(src, dst, send, recv, device):
    return pltpu.make_async_remote_copy(
        src_ref=src,
        dst_ref=dst,
        send_sem=send,
        recv_sem=recv,
        device_id=(device,),
        device_id_type=MESH,
    )


def greet(device):
    pl.semaphore_signal(
        pltpu.get_barrier_semaphore(), inc=1, device_id=(device,), device_id_type=MESH
    )


def normalize(values):
    centred = values - jnp.mean(values, -1, keepdims=True)
    scale = lax.rsqrt(jnp.mean(centred * centred, -1, keepdims=True) + 1e-05)
    return centred * scale, scale


def norm_back(grad, hat, scale):
    mean_one = jnp.mean(grad, -1, keepdims=True)
    mean_two = jnp.mean(grad * hat, -1, keepdims=True)
    return scale * (grad - mean_one - hat * mean_two)


class Gather:
    def __init__(self, r):
        self.r = r
        self.me, self.z, self.y, self.x, self.c = place()

    def hop(self, k, step, part, device):
        return link(part, part, self.r.gsend.at[k, step], self.r.grecv.at[k, step], device)

    def along_z(self, k, step):
        part = self.r.wire.at[self.z, self.y, self.x, self.c, pl.ds(*PIECES[k])]
        return self.hop(k, step, part, device_at((self.z + step + 1) % 4, self.y, self.x, self.c))

    def from_z(self, k, step):
        there = (self.z + 3 - step) % 4
        part = self.r.wire.at[there, self.y, self.x, self.c, pl.ds(*PIECES[k])]
        return self.hop(k, step, part, device_at(there, self.y, self.x, self.c))

    def plane(self, k, second, mine):
        z, y, x, c = self.z, self.y, self.x, self.c
        rows, wire = pl.ds(*PIECES[k]), self.r.wire
        py, px = (y, x) if mine else (1 - y, 1 - x)
        along_x = PIECE_X_FIRST[k] == second
        if along_x:
            part = wire.at[:, y, px, c, rows] if second else wire.at[:, :, px, c, rows]
            return self.hop(k, 3 if second else 4, part, device_at(z, y, 1 - x, c))
        part = wire.at[:, py, x, c, rows] if second else wire.at[:, py, :, c, rows]
        return self.hop(k, 3 if second else 4, part, device_at(z, 1 - y, x, c))

    def core(self, k, mine):
        part = self.r.wire.at[:, :, :, self.c if mine else 1 - self.c, pl.ds(*PIECES[k])]
        return self.hop(k, 5, part, device_at(self.z, self.y, self.x, 1 - self.c))

    def first(self, *chunks):
        for k in chunks:
            for step in range(3):
                self.along_z(k, step).start()

    def second(self, *chunks):
        for k in chunks:
            for step in range(3):
                self.from_z(k, step).wait_recv()
            self.plane(k, True, True).start()

    def third(self, *chunks):
        for k in chunks:
            self.plane(k, True, False).wait_recv()
            self.plane(k, False, True).start()

    def fourth(self, *chunks):
        for k in chunks:
            self.plane(k, False, False).wait_recv()
            self.core(k, True).start()

    def last(self, *chunks):
        for k in chunks:
            self.core(k, False).wait_recv()

    def drain(self):
        for k in range(len(PIECES)):
            for step in range(3):
                self.along_z(k, step).wait_send()
            self.plane(k, True, True).wait_send()
            self.plane(k, False, True).wait_send()
            self.core(k, True).wait_send()

    def fill(self):
        r = self.r
        spot = (self.z, self.y, self.x, self.c)

        def tiles(source, m, base, number):
            for j in range(number):
                pair = [source[m, :, pl.ds((2 * j + k) * LANES, LANES)] for k in range(2)]
                r.wire[spot + (pl.ds(base + j * 16, 16),)] = jnp.concatenate(pair, axis=0).astype(BF16)

        for m in range(5):
            tiles(r.sqw_v, m, SQ_AT[m], 1)
        for m in range(2):
            tiles(r.mlpw_v, m, m * MLP_ROWS, 4)
        gains, edge = r.gain_v[...], r.edge
        high = gains.astype(BF16).astype(F32)
        middle = (gains - high).astype(BF16).astype(F32)
        edge[...] = jnp.zeros_like(edge)
        edge[0:2, 0:TILE] = high
        edge[2:4, 0:TILE] = middle
        edge[4:6, 0:TILE] = (gains - high - middle).astype(BF16).astype(F32)
        r.wire[spot + (pl.ds(GAIN_BASE, 16),)] = edge[...].astype(BF16)

    def unpack(self, base, number, out, m):
        for j in range(number):
            block = self.r.wire[:, :, :, :, pl.ds(base + j * 16, 16), :].reshape(32, 16, LANES).astype(F32)
            for half in range(2):
                columns = pl.ds((2 * j + half) * LANES, LANES)
                out[m, :, columns] = block[:, half * 8 : half * 8 + 8, :].reshape(256, LANES).astype(BF16)

    def unpack_gains(self):
        edge, wire = self.r.edge, self.r.wire
        for half in range(2):
            total = jnp.zeros((16, LANES), F32)
            for at in range(16):
                d = half * 16 + at
                tile = wire[d // 8, (d // 4) % 2, (d // 2) % 2, d % 2, pl.ds(GAIN_BASE, 16), :].astype(F32)
                total = total + (tile if at == 0 else pltpu.roll(tile, at * TILE, 1))
            edge[...] = total
            self.r.gain_all[:, pl.ds(half * LANES, LANES)] = edge[0:2, :] + edge[2:4, :] + edge[4:6, :]


class Update:
    def __init__(self, r):
        self.r = r
        self.me, self.z, self.y, self.x, self.c = place()

    def hop(self, k, step, src, dst, device):
        return link(src, dst, self.r.send.at[k, step], self.r.recv.at[k, step], device)

    def core(self, k):
        rows = pl.ds(*CHUNKS[k])
        src, dst = self.r.send0.at[:, :, :, rows], self.r.got_core.at[:, :, :, rows]
        return self.hop(k, 0, src, dst, device_at(self.z, self.y, self.x, 1 - self.c))

    def plane(self, k, first):
        rows = pl.ds(*CHUNKS[k])
        to = (self.z, self.y, 1 - self.x, self.c) if X_FIRST[k] == first else (self.z, 1 - self.y, self.x, self.c)
        if first:
            src, dst = self.r.send1.at[:, :, rows], self.r.got1.at[:, :, rows]
        else:
            src, dst = self.r.send2.at[:, rows], self.r.got2.at[:, rows]
        return self.hop(k, 1 if first else 2, src, dst, device_at(*to))

    def along_z(self, k, step):
        rows = pl.ds(*CHUNKS[k])
        there = (self.z + step + 1) % 4
        src, dst = self.r.send3.at[there, rows], self.r.got3.at[step, rows]
        return self.hop(k, 3 + step, src, dst, device_at(there, self.y, self.x, self.c))

    def start(self, k):
        rows = pl.ds(*CHUNKS[k])
        self.r.send0[:, :, :, rows, :] = self.r.grads[:, :, :, 1 - self.c, rows, :].astype(BF16)
        self.core(k).start()

    def one(self, *chunks):
        r = self.r
        for k in chunks:
            rows = pl.ds(*CHUNKS[k])
            self.core(k).wait_recv()
            sum1 = r.sum1
            sum1[:, :, :, rows, :] = r.grads[:, :, :, self.c, rows, :] + r.got_core[:, :, :, rows, :].astype(F32)
            other = sum1[:, :, 1 - self.x, rows, :] if X_FIRST[k] else sum1[:, 1 - self.y, :, rows, :]
            r.send1[:, :, rows, :] = other.astype(BF16)
            self.plane(k, True).start()

    def two(self, *chunks):
        r = self.r
        for k in chunks:
            rows = pl.ds(*CHUNKS[k])
            self.plane(k, True).wait_recv()
            sum1, sum2 = r.sum1, r.sum2
            mine = sum1[:, :, self.x, rows, :] if X_FIRST[k] else sum1[:, self.y, :, rows, :]
            sum2[:, :, rows, :] = mine + r.got1[:, :, rows, :].astype(F32)
            other = 1 - self.y if X_FIRST[k] else 1 - self.x
            r.send2[:, rows, :] = sum2[:, other, rows, :].astype(BF16)
            self.plane(k, False).start()

    def three(self, *chunks):
        r = self.r
        for k in chunks:
            rows = pl.ds(*CHUNKS[k])
            self.plane(k, False).wait_recv()
            mine = self.y if X_FIRST[k] else self.x
            total = r.sum2[:, mine, rows, :] + r.got2[:, rows, :].astype(F32)
            r.sum3[:, rows, :] = total
            r.send3[:, rows, :] = total.astype(BF16)
            if k >= 4:
                own = r.sum3[self.z, rows, :] + 0.5 * r.moment[rows, :]
                r.send3[self.z, rows, :] = own.astype(BF16)
                self.parts_to_owners(k)
            for step in range(3):
                self.along_z(k, step).start()

    def parts_to_owners(self, k):
        for part, (chunk, index, *_) in enumerate(PARTS_OUT):
            if chunk != k:
                continue

            @pl.when(self.me != OWNERS[index])
            def _():
                self.to_owner(part).start()

            @pl.when(self.me == OWNERS[index])
            def _():
                src, dst = self.own_part(part)
                pltpu.make_async_copy(src, dst, self.r.own_recv.at[0]).start()

    def result(self, index):
        return self.r.result_mlp if index < 2 else self.r.result_sq

    def own_part(self, part):
        _, index, base, number, place = PARTS_OUT[part]
        if index < 2:
            return self.r.moment_low.at[pl.ds(base, number)], self.r.slabs_mlp.at[self.me, pl.ds(place, number)]
        return self.r.send3.at[:, pl.ds(base, number)], self.r.slabs_sq.at[self.z, self.me % 8]

    def to_owner(self, part):
        src, dst = self.own_part(part)
        return link(src, dst, self.r.own_send.at[part], self.r.own_recv.at[0], OWNERS[PARTS_OUT[part][1]])

    def four(self, *chunks):
        r = self.r
        moment, out = r.moment, r.out
        for k in chunks:
            rows = pl.ds(*CHUNKS[k])
            total = r.sum3[self.z, rows, :]
            for step in range(3):
                self.along_z(k, step).wait_recv()
                total = total + r.got3[step, rows, :].astype(F32)
            out[0, rows, :] = total
            new = 0.5 * moment[rows, :] + total
            moment[rows, :] = new
            if k < 4:
                r.moment_low[rows, :] = new.astype(BF16)
            if k < 4:
                self.parts_to_owners(k)

    def old_moment(self):
        r = self.r
        moment = r.moment
        for m in range(2):
            for j in range(8):
                moment[pl.ds(m * MLP_ROWS + j * TILE, TILE), :] = r.mlpm_v[m, :, pl.ds(j * LANES, LANES)]
        for m in range(5):
            for j in range(2):
                moment[pl.ds(SQ_AT[m] + j * TILE, TILE), :] = r.sqm_v[m, :, pl.ds(j * LANES, LANES)]
        moment[pl.ds(GAIN_BASE, 16), :] = jnp.zeros((16, LANES), F32)

    def orthogonalize(self):
        r = self.r
        cur = r.cur
        rows = lax.broadcasted_iota(jnp.int32, (256, 256), 0)
        diagonal = rows == lax.broadcasted_iota(jnp.int32, (256, 256), 1)

        low = r.cur_low

        def load(rows, j, pair):
            for side in range(2):
                columns = pl.ds((2 * j + side) * LANES, LANES)
                part = pair[:, side * TILE : (side + 1) * TILE, :].reshape(-1, LANES)
                cur[rows, columns] = part
                low[rows, columns] = part.astype(BF16)

        def load_mlp():
            for j in range(4):
                load(pl.ds(0, 256), j, r.slabs_mlp[:, pl.ds(j * 16, 16), :].astype(F32))

        def load_sq():
            for to in range(4):
                pair = r.slabs_sq[0, :, to].astype(F32)
                for plane in range(1, 4):
                    pair = pair + r.slabs_sq[plane, :, to].astype(F32)
                load(pl.ds(to * 64, 64), 0, pair)

        def run(slabs, fetch, result, tiles):
            pltpu.make_async_copy(slabs, slabs, r.own_recv.at[0]).wait()
            fetch()
            scale = 1.0
            for turn, shift in enumerate(SHIFTS):
                whole = low[:, 0 : tiles * LANES]
                off = dot(whole, whole, NT)
                if turn == 0:
                    norm = jnp.sum(jnp.sum(jnp.where(diagonal, off, 0.0), axis=0, keepdims=True), axis=1, keepdims=True)
                    scale = 1.0 / (jnp.sqrt(norm) + 1e-07)
                    off = off * (scale * scale)
                if shift:
                    off = off - jnp.where(diagonal, shift, 0.0)
                off_low = off.astype(BF16)
                poly = (COEF_B + 2.0 * COEF_C * shift) * off + COEF_C * dot(off_low, off_low)
                poly = poly.astype(BF16)
                keep = COEF_A + shift * (COEF_B + COEF_C * shift)
                for j in range(tiles // 2):
                    columns = pl.ds(j * 2 * LANES, 2 * LANES)
                    now = keep * cur[:, columns] + dot(poly, low[:, columns])
                    if turn == 0:
                        now = now * scale
                    if turn < len(SHIFTS) - 1:
                        cur[:, columns] = now
                        low[:, columns] = now.astype(BF16)
                    else:
                        parts = [now[:, side * LANES : (side + 1) * LANES].reshape(32, TILE, LANES) for side in range(2)]
                        result[:, pl.ds(j * 16, 16), :] = jnp.concatenate(parts, axis=1).astype(result.dtype)

        mine_mlp = jnp.logical_or(self.me == OWNERS[0], self.me == OWNERS[1])
        mine_sq = self.me < 0
        for device in OWNERS[2:]:
            mine_sq = jnp.logical_or(mine_sq, self.me == device)

        @pl.when(mine_mlp)
        def _():
            run(r.slabs_mlp, load_mlp, r.result_mlp, 8)

        @pl.when(mine_sq)
        def _():
            run(r.slabs_sq, load_sq, r.result_sq, 2)

    def landing(self, index):
        if index < 2:
            return self.r.back_mlp.at[index]
        return self.r.back_sq.at[index - 2]

    def give_back(self, index, device):
        result = self.result(index)
        return link(
            result.at[device], self.landing(index),
            self.r.back_send.at[device], self.r.back_recv.at[index], device,
        )

    def give_all(self):
        r = self.r
        for index in range(7):
            result = self.result(index)

            @pl.when(self.me == OWNERS[index])
            def _():
                def send_one(step, _):
                    self.give_back(index, step + (step + 32 - self.me) // 32).start()
                    return 0

                lax.fori_loop(0, 31, send_one, 0)
                pltpu.make_async_copy(result.at[self.me], self.landing(index), r.back_recv.at[index]).start()

    def take_all(self):
        for index in range(7):
            result = self.result(index)
            pltpu.make_async_copy(result.at[0], self.landing(index), self.r.back_recv.at[index]).wait()
        for index in range(2):
            rows = pl.ds(index * MLP_ROWS, MLP_ROWS)
            self.r.out[2, rows, :] = self.r.back_mlp[index].astype(F32)
        for index in range(5):
            self.r.out[2, pl.ds(SQ_AT[index], SQ_ROWS), :] = self.r.back_sq[index].astype(F32)

    def drain(self):
        for k in range(len(CHUNKS)):
            self.core(k).wait_send()
            self.plane(k, True).wait_send()
            self.plane(k, False).wait_send()
            for step in range(3):
                self.along_z(k, step).wait_send()
        for part in range(len(PARTS_OUT)):

            @pl.when(self.me != OWNERS[PARTS_OUT[part][1]])
            def _():
                self.to_owner(part).wait_send()

    def drain_owner(self):
        for index in range(7):

            @pl.when(self.me == OWNERS[index])
            def _():
                def wait_one(step, _):
                    self.give_back(index, step + (step + 32 - self.me) // 32).wait_send()
                    return 0

                lax.fori_loop(0, 31, wait_one, 0)


def greet_all():
    me, z, y, x, c = place()
    greet(device_at(z, y, x, 1 - c))
    greet(device_at(z, y, 1 - x, c))
    greet(device_at(z, 1 - y, x, c))
    for step in range(1, 4):
        greet(device_at((z + step) % 4, y, x, c))
    owner = me < 0
    for device in OWNERS:
        owner = jnp.logical_or(owner, me == device)

        @pl.when(me != device)
        def _():
            greet(device)

    @pl.when(owner)
    def _():
        def greet_other(step, _):
            greet((me + step) % 32)
            return 0

        lax.fori_loop(1, 32, greet_other, 0)

    is_owner = owner.astype(jnp.int32)
    return 6 + 7 - is_owner + 31 * is_owner


def block_kernel(names, remote, *args):
    r = Refs(zip(names, args))
    keys, samples = r.obs.shape[0], r.obs.shape[1]
    tokens, width = r.acts.shape
    head_dim, half, per = width // HEADS, width // 2, ROWS // ACT
    wide = r.mlp_all.shape[2]
    groups = samples // GROUP
    in_sems, out_sems = r.in_sems, r.out_sems

    if remote:
        own = (r.sqw_v, r.mlpw_v, r.gain_v)
    else:
        own = (r.sq_all, r.mlp_all, r.gain_all)
    loads = list(zip((r.sqw, r.mlpw, r.gain), own))
    loads += [(r.acts, r.acts_v), (r.obs, r.obs_v.at[pl.ds(0, keys)]), (r.cot, r.cot_v)]
    if remote:
        loads += [(r.sqm, r.sqm_v), (r.mlpm, r.mlpm_v)]
    loads += [(r.flags, r.flags_s), (r.levels, r.levels_s)]
    copies = [pltpu.make_async_copy(a, b, in_sems.at[i]) for i, (a, b) in enumerate(loads)]

    def arrive(*which):
        for i in which:
            copies[i].wait()

    for copy in copies:
        copy.start()
    if remote:
        gather, update = Gather(r), Update(r)
        expected = greet_all()
        arrive(0, 1, 2)
        gather.fill()
        pl.semaphore_wait(pltpu.get_barrier_semaphore(), expected)
        gather.first(5, 6, 4, 0, 1, 2, 3)

    arrive(3)

    def hats(i, _):
        rows = pl.ds(pl.multiple_of(i * ROWS, ROWS), ROWS)
        hat, scale = normalize(r.acts_v[rows, :])
        r.xhat[rows, :] = hat
        r.rstd[rows, :] = scale
        return 0

    lax.fori_loop(0, tokens // ROWS, hats, 0)

    mem, obs_v = r.mem, r.obs_v
    batch = 16
    chunks = KEYS_PAD // batch
    swap = r.swap
    row = lax.broadcasted_iota(jnp.int32, swap.shape, 0)
    column = lax.broadcasted_iota(jnp.int32, swap.shape, 1)
    swap[...] = jnp.where(column == (row % batch) * batch + row // batch, 1.0, 0.0).astype(BF16)

    def turn(part, low, high):
        def one(j, _):
            at = pl.ds(pl.multiple_of(j * batch, batch), batch)
            here = pl.ds(part * batch, batch)
            block = obs_v[at, here, :].reshape(batch * batch, width)
            mem[here, at, :] = dot(swap[...], block).astype(BF16).reshape(batch, batch, width)
            return 0

        lax.fori_loop(low, high, one, 0, unroll=high - low)

    whole = chunks - 1
    arrive(4)
    turn(0, 0, whole // 2)
    if remote:
        gather.second(5, 6)
    turn(0, whole // 2, whole)
    if remote:
        gather.third(5, 6)
    turn(1, 0, whole // 2)
    if remote:
        gather.second(4, 0, 1)
        gather.fourth(5, 6)
    turn(1, whole // 2, whole)
    if remote:
        gather.second(2, 3)
    arrive(len(copies) - 1, len(copies) - 2)
    freqs = jnp.exp(
        lax.broadcasted_iota(jnp.int32, (1, half), 1).astype(F32) * F32(-math.log(10000.0)) / half
    )
    for s in range(samples):
        r.angle[s : s + 1, :] = r.levels_s[s].astype(F32) * freqs
    r.embed[:, 0:half] = jnp.sin(r.angle[...]).astype(BF16)
    r.embed[:, half:width] = jnp.cos(r.angle[...]).astype(BF16)
    if remote:
        arrive(6, 7)
        update.old_moment()
        gather.third(4, 0, 1)
        gather.last(5, 6)
        for m in range(3):
            gather.unpack(SQ_AT[m], 1, r.sq_all, m)
        gather.unpack_gains()
    else:
        arrive(0, 1, 2)

    sq, mlp = r.sq_all, r.mlp_all
    wkh, wvh = r.wkh, r.wvh
    lane = lax.broadcasted_iota(jnp.int32, (width, width), 1)

    def split_heads(out, weight):
        weight = weight.astype(F32)
        for h in range(HEADS):
            out[pl.ds(h * width, width), :] = jnp.where(lane // head_dim == h, weight, 0.0).astype(BF16)

    split_heads(wkh, sq[2])
    g1, g2 = r.gain_all[0:1, :], r.gain_all[1:2, :]

    obs_v[keys] = dot(r.embed[...], sq[0]).astype(BF16)
    obs_v[keys + 1 :] = jnp.zeros((KEYS_PAD - keys - 1, samples, width), BF16)
    for part in range(samples // batch):
        turn(part, whole, chunks)

    sides, weights = r.sides_v, r.pds_v

    def make_queries(i, _):
        rows = pl.ds(pl.multiple_of(i * ROWS, ROWS), ROWS)
        first = (r.xhat[rows, :] * g1).astype(BF16)
        r.first[rows, :] = first
        q = dot(first, sq[1]).astype(BF16)
        r.query[rows, :] = q
        here = pl.ds(i * per, per)
        for h in range(HEADS):
            wk = wkh[pl.ds(h * width, width), :]
            value = (dot(q, wk, NT) * 0.125).astype(BF16).reshape(per, ACT, width)
            sides[here, pl.ds((HEADS + h) * ACT, ACT), :] = value
        return 0

    lax.fori_loop(0, tokens // ROWS, make_queries, 0)

    key = lax.broadcasted_iota(jnp.int32, (1, KEYS_PAD), 1)
    low_rows, high_rows = pl.ds(0, HEADS * ACT), pl.ds(HEADS * ACT, HEADS * ACT)

    def attend(g, _):
        ids = [g * GROUP + k for k in range(GROUP)]
        scores = [dot(sides[s, high_rows, :], mem[s], NT) for s in ids]
        lows = []
        for s, score in zip(ids, scores):
            count = OBS_FEW + (OBS_FULL - OBS_FEW) * r.flags_s[s]
            score = score + jnp.where((key < count) | (key == OBS_FULL), 0.0, -1000000000.0)
            expo = jnp.exp(score - jnp.max(score, -1, keepdims=True))
            probs = expo * (1.0 / jnp.sum(expo, -1, keepdims=True))
            r.probs[s] = probs
            low = probs.astype(BF16)
            weights[s, low_rows, :] = low
            lows.append(low)
        for s, low in zip(ids, lows):
            u = dot(low, mem[s]).astype(BF16)
            rows = pl.ds(pl.multiple_of(s * ACT, ACT), ACT)
            for h in range(HEADS):
                r.u[rows, pl.ds(h * width, width)] = u[h * ACT : (h + 1) * ACT, :]
        return 0

    lax.fori_loop(0, groups // 2, attend, 0)
    if remote:
        gather.third(2, 3)
        gather.fourth(4, 0, 1)
    lax.fori_loop(groups // 2, groups, attend, 0)
    if remote:
        gather.fourth(2, 3)
        gather.last(4)
        for m in range(3, 5):
            gather.unpack(SQ_AT[m], 1, sq, m)
    split_heads(wvh, sq[3])

    gain_acc = r.gain_acc
    gain_acc[...] = jnp.zeros_like(gain_acc)
    blocks = [pl.ds(i * ROWS, ROWS) for i in range(tokens // ROWS)]
    for rows in blocks:
        mixed = dot(r.u[rows, :], wvh[...]).astype(BF16)
        r.mixed[rows, :] = mixed
        resid = r.acts_v[rows, :] + dot(mixed, sq[4])
        r.resid[rows, :] = resid
        hat, scale = normalize(resid)
        r.hat_two[rows, :] = hat
        r.rstd_two[rows, :] = scale
        r.second[rows, :] = (hat * g2).astype(BF16)
    arrive(5)
    r.out_low[...] = r.cot_v[...].astype(BF16)
    if remote:
        gather.last(0, 1)
        gather.unpack(0, 4, mlp, 0)
    wide_blocks = [pl.ds(c * 256, 256) for c in range(wide // 256)]
    for rows in blocks:
        for columns in wide_blocks:
            v = dot(r.second[rows, :], mlp[0, :, columns])
            square = v * v
            t = jnp.tanh(0.7978845608 * (v + 0.044715 * square * v))
            r.active[rows, columns] = (0.5 * v * (1.0 + t)).astype(BF16)
            slope = 0.5 * (1.0 + t) + 0.5 * v * (1.0 - t * t) * (0.7978845608 * (1.0 + 0.134145 * square))
            r.slope[rows, columns] = slope

    grads = r.grads

    def put(base, tiles, value):
        for j in range(tiles):
            part = value[:, j * LANES : (j + 1) * LANES].reshape(GRID + (TILE, LANES))
            grads[:, :, :, :, pl.ds(base + j * TILE, TILE), :] = part

    def by_head(left, right):
        turned = left.T
        parts = [
            dot(turned[h * head_dim : (h + 1) * head_dim, :], right[:, pl.ds(h * width, width)])
            for h in range(HEADS)
        ]
        return jnp.concatenate(parts, axis=0).T

    put(MLP_ROWS, 8, dot(r.out_low[...], r.active[...], TN))
    if remote:
        update.start(2)
        update.start(3)
        gather.last(2, 3)
        gather.unpack(MLP_ROWS, 4, mlp, 1)
    for rows in blocks:
        for columns in wide_blocks:
            slope = r.slope[rows, columns]
            r.dhidden[rows, columns] = (slope * dot(r.out_low[rows, :], mlp[1, :, columns])).astype(BF16)
    put(0, 8, dot(r.second[...], r.dhidden[...], TN))
    if remote:
        update.start(0)
        update.start(1)
        update.one(2, 3)
    for i, rows in enumerate(blocks):
        r.out_v[rows, :] = r.resid[rows, :] + dot(r.active[rows, :], mlp[1], NT)
        grad_second = dot(r.dhidden[rows, :], mlp[0], NT)
        hat = r.hat_two[rows, :]
        gain_acc[1:2, :] += jnp.sum(grad_second * hat, 0, keepdims=True)
        dres = r.cot_v[rows, :] + norm_back(grad_second * g2, hat, r.rstd_two[rows, :])
        r.dres[rows, :] = dres
        low = dres.astype(BF16)
        r.dres_low[rows, :] = low
        gm = dot(low, sq[4], NT).astype(BF16)
        r.dmixed[rows, :] = gm
        here = pl.ds(i * per, per)
        for h in range(HEADS):
            wv = wvh[pl.ds(h * width, width), :]
            sides[here, pl.ds(h * ACT, ACT), :] = dot(gm, wv, NT).astype(BF16).reshape(per, ACT, width)
    keep_out = pltpu.make_async_copy(r.out_v, r.output, out_sems.at[0])
    keep_out.start()
    if remote:
        update.one(0, 1)
    put(SQ_AT[4], 2, dot(r.mixed[...], r.dres_low[...], TN))
    put(SQ_AT[3], 2, by_head(r.dmixed[...], r.u))
    if remote:
        update.start(4)

    def attend_back(g, _):
        ids = [g * GROUP + k for k in range(GROUP)]
        rises = [dot(sides[s, low_rows, :], mem[s], NT) for s in ids]
        for s, rise in zip(ids, rises):
            probs = r.probs[s]
            both = probs * rise
            weights[s, high_rows, :] = (both - probs * jnp.sum(both, -1, keepdims=True)).astype(BF16)
        for s in ids:
            dq = (dot(weights[s, high_rows, :], mem[s]) * 0.125).astype(BF16)
            rows = pl.ds(pl.multiple_of(s * ACT, ACT), ACT)
            for h in range(HEADS):
                r.dq_wide[rows, pl.ds(h * width, width)] = dq[h * ACT : (h + 1) * ACT, :]
            end = dot(weights[s, :, LANES:KEYS_PAD], sides[s], TN)
            r.stamps[s] = end[64:72, :]
        return 0

    lax.fori_loop(0, groups // 2, attend_back, 0)
    if remote:
        update.two(2, 3)
        update.one(4)
        update.two(0, 1)
    lax.fori_loop(groups // 2, groups, attend_back, 0)
    if remote:
        update.three(2, 3)
        update.two(4)
    put(SQ_AT[2], 2, by_head(r.query[...], r.dq_wide))
    stamp_low = r.stamps[:, 4:5, :].reshape(samples, width).astype(BF16)
    put(SQ_AT[0], 2, dot(r.embed[...], stamp_low, TN))
    if remote:
        update.start(5)
        update.three(0, 1)

    def memory_back(low, high):
        for s in range(2 * low, 2 * high):
            mem[s] = dot(weights[s], sides[s], TN).astype(BF16)

    def keep_og(part):
        here = pl.ds(part * batch, batch)
        return pltpu.make_async_copy(obs_v.at[pl.ds(0, keys), here], r.og.at[:, here], out_sems.at[2 + part])

    def turn_back(part, low, high):
        def one(j):
            at = pl.ds(pl.multiple_of(j * batch, batch), batch)
            here = pl.ds(part * batch, batch)
            block = mem[here, at, :].reshape(batch * batch, width)
            value = dot(swap[...], block).astype(BF16).reshape(batch, batch, width)
            obs_v[at, here, :] = value

        for j in range(low, high):
            one(j)
        if high == chunks:
            keep_og(part).start()

    def queries_back(i, _):
        rows = pl.ds(pl.multiple_of(i * ROWS, ROWS), ROWS)
        r.dquery[rows, :] = dot(r.dq_wide[rows, :], wkh[...]).astype(BF16)
        return 0

    lax.fori_loop(0, tokens // ROWS, queries_back, 0)
    put(SQ_AT[1], 2, dot(r.first[...], r.dquery[...], TN))
    if remote:
        update.start(6)
        update.one(5)

    def acts_back(i, _):
        rows = pl.ds(pl.multiple_of(i * ROWS, ROWS), ROWS)
        grad_first = dot(r.dquery[rows, :], sq[1], NT)
        hat = r.xhat[rows, :]
        gain_acc[0:1, :] += jnp.sum(grad_first * hat, 0, keepdims=True)
        r.ag_v[rows, :] = r.dres[rows, :] + norm_back(grad_first * g1, hat, r.rstd[rows, :])
        return 0

    def finish_acts():
        lax.fori_loop(0, tokens // ROWS, acts_back, 0)
        for norm in range(2):
            for j in range(2):
                row = gain_acc[norm : norm + 1, j * LANES : (j + 1) * LANES]
                at = GAIN_BASE + norm * 2 + j
                value = jnp.broadcast_to(row.reshape(1, 1, 1, 1, 1, LANES), GRID + (1, LANES))
                grads[:, :, :, :, at : at + 1, :] = value
        rest = WIRE - GAIN_BASE - 4
        grads[:, :, :, :, GAIN_BASE + 4 : WIRE, :] = jnp.zeros(GRID + (rest, LANES), F32)

    keep_ag = pltpu.make_async_copy(r.ag_v, r.ag, out_sems.at[1])
    if remote:
        pairs = samples // 2
        finish_acts()
        keep_ag.start()
        update.start(7)
        update.one(6)
        update.three(4)
        memory_back(0, pairs // 2)
        update.four(2, 3)
        update.two(5)
        update.one(7)
        update.two(6)
        memory_back(pairs // 2, pairs)
        update.four(0, 1)
        update.three(5)
        update.two(7)
        update.three(6)
        turn_back(0, 0, chunks // 2)
        update.orthogonalize()
        update.give_all()
        update.three(7)
        turn_back(0, chunks // 2, chunks)
        update.four(4, 5, 6)
        turn_back(1, 0, chunks)
        update.four(7)
        out = r.out
        out[1, :, :] = r.moment[...]
        out[2, pl.ds(GAIN_BASE, 16), :] = jnp.zeros((16, LANES), F32)
        gather.drain()
        update.drain()
        update.take_all()
        update.drain_owner()
    else:
        finish_acts()
        keep_ag.start()
        memory_back(0, samples // 2)
        for part in range(samples // batch):
            turn_back(part, 0, chunks)
    for copy in (keep_out, keep_ag, *(keep_og(part) for part in range(samples // batch))):
        copy.wait()


def block_and_back(remote, acts, obs, flags, levels, cot, sqw, mlpw, gain, sqm=None, mlpm=None):
    tokens, width = acts.shape
    keys, samples = obs.shape[0], obs.shape[1]
    rows = HEADS * ACT
    wide = mlpw.shape[2]
    any_space = pl.BlockSpec(memory_space=pl.ANY)
    in_vmem = pl.BlockSpec(memory_space=VMEM)
    sem = pltpu.SemaphoreType.DMA
    ins = dict(flags=flags, levels=levels, acts=acts, obs=obs, cot=cot, sqw=sqw, mlpw=mlpw, gain=gain)
    outs = dict(
        output=jax.ShapeDtypeStruct(acts.shape, F32),
        ag=jax.ShapeDtypeStruct(acts.shape, F32),
        og=jax.ShapeDtypeStruct(obs.shape, BF16),
    )
    grads = GRID + (WIRE, LANES)
    scratch = dict(
        obs_v=VMEM((KEYS_PAD, samples, width), BF16),
        acts_v=VMEM(acts.shape, F32),
        cot_v=VMEM(acts.shape, F32),
        mem=VMEM((samples, KEYS_PAD, width), BF16),
        swap=VMEM((256, 256), BF16),
        sq_all=VMEM((5, width, width), BF16),
        mlp_all=VMEM((2, width, wide), BF16),
        gain_all=VMEM((2, width), F32),
        wkh=VMEM((HEADS * width, width), BF16),
        wvh=VMEM((HEADS * width, width), BF16),
        first=VMEM((tokens, width), BF16),
        query=VMEM((tokens, width), BF16),
        xhat=VMEM((tokens, width), F32),
        rstd=VMEM((tokens, 1), F32),
        probs=VMEM((samples, rows, KEYS_PAD), F32),
        pds_v=VMEM((samples, 2 * rows, KEYS_PAD), BF16),
        sides_v=VMEM((samples, 2 * rows, width), BF16),
        u=VMEM((tokens, HEADS * width), BF16),
        dq_wide=VMEM((tokens, HEADS * width), BF16),
        mixed=VMEM((tokens, width), BF16),
        second=VMEM((tokens, width), BF16),
        active=VMEM((tokens, wide), BF16),
        dhidden=VMEM((tokens, wide), BF16),
        out_low=VMEM((tokens, width), BF16),
        dres_low=VMEM((tokens, width), BF16),
        dres=VMEM((tokens, width), F32),
        resid=VMEM((tokens, width), F32),
        hat_two=VMEM((tokens, width), F32),
        rstd_two=VMEM((tokens, 1), F32),
        slope=VMEM((tokens, wide), F32),
        dmixed=VMEM((tokens, width), BF16),
        dquery=VMEM((tokens, width), BF16),
        out_v=VMEM((tokens, width), F32),
        ag_v=VMEM((tokens, width), F32),
        angle=VMEM((samples, width // 2), F32),
        embed=VMEM((samples, width), BF16),
        stamps=VMEM((samples, 8, width), F32),
        gain_acc=VMEM((8, width), F32),
        flags_s=pltpu.SMEM(flags.shape, jnp.int32),
        levels_s=pltpu.SMEM(levels.shape, jnp.int32),
        in_sems=sem((10,)),
        out_sems=sem((2 + samples // 16,)),
    )
    extra = {}
    if remote:
        ins.update(sqm=sqm, mlpm=mlpm)
        outs.update(out=jax.ShapeDtypeStruct((3, WIRE, LANES), F32))
        chunks = len(CHUNKS)
        scratch.update(
            grads=VMEM(grads, F32),
            sqw_v=VMEM(sqw.shape, F32),
            mlpw_v=VMEM(mlpw.shape, F32),
            gain_v=VMEM(gain.shape, F32),
            sqm_v=VMEM(sqm.shape, F32),
            mlpm_v=VMEM(mlpm.shape, F32),
            wire=VMEM(grads, BF16),
            edge=VMEM((16, LANES), F32),
            gsend=sem((len(PIECES), 6)),
            grecv=sem((len(PIECES), 6)),
            send0=VMEM((4, 2, 2, WIRE, LANES), BF16),
            got_core=VMEM((4, 2, 2, WIRE, LANES), BF16),
            sum1=VMEM((4, 2, 2, WIRE, LANES), F32),
            send1=VMEM((4, 2, WIRE, LANES), BF16),
            got1=VMEM((4, 2, WIRE, LANES), BF16),
            sum2=VMEM((4, 2, WIRE, LANES), F32),
            send2=VMEM((4, WIRE, LANES), BF16),
            got2=VMEM((4, WIRE, LANES), BF16),
            sum3=VMEM((4, WIRE, LANES), F32),
            send3=VMEM((4, WIRE, LANES), BF16),
            got3=VMEM((3, WIRE, LANES), BF16),
            moment=VMEM((WIRE, LANES), F32),
            slabs_sq=VMEM((4, 8, 4, SQ_ROWS, LANES), BF16),
            slabs_mlp=VMEM((32, MLP_ROWS, LANES), BF16),
            moment_low=VMEM((2 * MLP_ROWS, LANES), BF16),
            back_mlp=VMEM((2, MLP_ROWS, LANES), BF16),
            back_sq=VMEM((5, SQ_ROWS, LANES), BF16),
            result_sq=VMEM((32, SQ_ROWS, LANES), BF16),
            result_mlp=VMEM((32, MLP_ROWS, LANES), BF16),
            cur=VMEM((width, wide), F32),
            cur_low=VMEM((width, wide), BF16),
            send=sem((chunks, 6)),
            recv=sem((chunks, 6)),
            own_send=sem((len(PARTS_OUT),)),
            own_recv=sem((1,)),
            back_send=sem((32,)),
            back_recv=sem((7,)),
        )
        extra = dict(collective_id=0, has_side_effects=True)
        outs = {name: VMEM(like.shape, like.dtype) for name, like in outs.items()}
    else:
        outs.update(grads=jax.ShapeDtypeStruct(grads, F32))
    names = tuple(ins) + tuple(outs) + tuple(scratch)
    stay = [pltpu.with_memory_space_constraint(value, pltpu.HBM) for value in ins.values()]
    results = pl.pallas_call(
        functools.partial(block_kernel, names, remote),
        out_shape=tuple(outs.values()),
        in_specs=[any_space] * len(ins),
        out_specs=[any_space] * 3 + [in_vmem],
        scratch_shapes=list(scratch.values()),
        compiler_params=pltpu.CompilerParams(vmem_limit_bytes=52 << 20, **extra),
        name="block_and_back",
    )(*stay)
    return Refs(zip(outs, results))


PARTS = 7


def finish_kernel(names, rate, *args):
    r = Refs(zip(names, args))
    sems = r.sems
    keys = r.og.shape[0]
    step = keys // PARTS

    def leave(part):
        block = pl.ds(part * step, step)
        return pltpu.make_async_copy(r.og_v.at[block], r.og.at[block], sems.at[part])

    more = PARTS
    moves = []
    if hasattr(r, "wire"):
        pairs = [(r.sqw, r.sqw_v), (r.mlpw, r.mlpw_v), (r.gain, r.gain_v), (r.gainm, r.gainm_v)]
        pairs += [(r.output, r.output_f), (r.ag, r.ag_f)]
        for source, target in pairs:
            moves.append(pltpu.make_async_copy(source, target, sems.at[more]))
            moves[-1].start()
            more += 1
    for part in range(PARTS):

        def widen(j, _):
            r.og_v[j] = r.low[j].astype(F32)
            return 0

        lax.fori_loop(part * step, (part + 1) * step, widen, 0, unroll=4)
        leave(part).start()
    for copy in moves[:4]:
        copy.wait()
    if hasattr(r, "wire"):
        finish_weights(r, rate)
    for part in range(PARTS):
        leave(part).wait()
    for copy in moves[4:]:
        copy.wait()


def finish_weights(r, rate):
    wire = r.wire
    me = lax.axis_index("dp")
    for m in range(5):
        for j in range(2):
            rows, columns = pl.ds(SQ_AT[m] + j * TILE, TILE), pl.ds(j * LANES, LANES)
            r.sqg[m, :, columns] = wire[0, rows, :]
            r.sqm[m, :, columns] = wire[1, rows, :]
            r.sqn[m, :, columns] = r.sqw_v[m, :, columns] - SQ_RATES[m] * wire[2, rows, :]
    r.sqc[...] = r.sqn[...].astype(BF16)
    for m in range(2):
        for j in range(8):
            rows, columns = pl.ds(m * MLP_ROWS + j * TILE, TILE), pl.ds(j * LANES, LANES)
            r.mlpg[m, :, columns] = wire[0, rows, :]
            r.mlpm[m, :, columns] = wire[1, rows, :]
            r.mlpn[m, :, columns] = r.mlpw_v[m, :, columns] - MLP_RATES[m] * wire[2, rows, :]
    r.mlpc[...] = r.mlpn[...].astype(BF16)
    tile = wire[0, pl.ds(GAIN_BASE, TILE), :]
    turned = pltpu.roll(tile, (LANES - (me % 16) * TILE) % LANES, 1)
    at = me // 16
    for norm in range(2):
        pair = turned[2 * norm : 2 * norm + 2, 0:TILE]
        row = jnp.where(at == 0, pair[0:1, :], pair[1:2, :])
        new = 0.5 * r.gainm_v[norm : norm + 1, :] + row
        r.gg[norm : norm + 1, :] = row
        r.gm[norm : norm + 1, :] = new
        r.gn[norm : norm + 1, :] = r.gain_v[norm : norm + 1, :] - rate * new


def finish(rate, made, sqw=None, mlpw=None, gain=None, gainm=None):
    any_space = pl.BlockSpec(memory_space=pl.ANY)
    in_vmem = pl.BlockSpec(memory_space=VMEM)
    ins = dict(low=made.og)
    outs = dict(og=jax.ShapeDtypeStruct(made.og.shape, F32))
    near, far = 1, 1
    if hasattr(made, "out"):
        ins.update(output=made.output, ag=made.ag, wire=made.out, sqw=sqw, mlpw=mlpw, gain=gain, gainm=gainm)
        like = jax.ShapeDtypeStruct
        near, far = 4, 3
        outs.update(
            output_f=like(made.output.shape, F32),
            ag_f=like(made.ag.shape, F32),
            sqg=like(sqw.shape, F32),
            sqm=like(sqw.shape, F32),
            sqn=like(sqw.shape, F32),
            sqc=like(sqw.shape, BF16),
            mlpg=like(mlpw.shape, F32),
            mlpm=like(mlpw.shape, F32),
            mlpn=like(mlpw.shape, F32),
            mlpc=like(mlpw.shape, BF16),
            gg=like(gain.shape, F32),
            gm=like(gain.shape, F32),
            gn=like(gain.shape, F32),
        )
    scratch = dict(
        og_v=VMEM(made.og.shape, F32),
        sems=pltpu.SemaphoreType.DMA((PARTS + 6,)),
    )
    if hasattr(made, "out"):
        scratch.update(
            sqw_v=VMEM(sqw.shape, F32),
            mlpw_v=VMEM(mlpw.shape, F32),
            gain_v=VMEM(gain.shape, F32),
            gainm_v=VMEM(gainm.shape, F32),
        )
    names = tuple(ins) + tuple(outs) + tuple(scratch)
    made_here = list(ins.values())
    stay = [pltpu.with_memory_space_constraint(value, pltpu.HBM) for value in made_here[near:]]
    results = pl.pallas_call(
        functools.partial(finish_kernel, names, rate),
        out_shape=tuple(outs.values()),
        in_specs=[in_vmem] * near + [any_space] * (len(ins) - near),
        out_specs=[any_space] * far + [in_vmem] * (len(outs) - far),
        scratch_shapes=list(scratch.values()),
        compiler_params=pltpu.CompilerParams(vmem_limit_bytes=16 << 20),
        name="finish",
    )(*made_here[:near], *stay)
    return Refs(zip(outs, results))


HIGH_PRECISION = lax.Precision.HIGHEST


def plain_orthogonalize(matrix):
    current = matrix / (jnp.sqrt(jnp.sum(matrix * matrix)) + 1e-07)
    for turn in range(5):
        gram = jnp.dot(current, current.T, precision=HIGH_PRECISION)
        poly = COEF_B * gram + COEF_C * jnp.dot(gram, gram, precision=HIGH_PRECISION)
        current = COEF_A * current + jnp.dot(poly, current, precision=HIGH_PRECISION)
    return current


def pick_owned(stack, owners, device):
    chosen = jnp.zeros_like(stack[0])
    for index in range(len(owners)):
        chosen = jnp.where(device == owners[index], stack[index], chosen)
    return chosen


def is_owner(owners, device):
    flag = device < 0
    for owner in owners:
        flag = jnp.logical_or(flag, device == owner)
    return flag


def from_wire(grads):
    def matrix(base, tiles):
        part = grads[:, base : base + tiles * TILE, :].reshape(-1, tiles, TILE, LANES)
        return part.transpose(0, 2, 1, 3).reshape(-1, tiles * LANES)

    square = jnp.stack([matrix(SQ_AT[m], 2) for m in range(5)])
    mlp = jnp.stack([matrix(m * MLP_ROWS, 8) for m in range(2)])
    return square, mlp, grads[0, GAIN_BASE : GAIN_BASE + 4, :].reshape(2, 2 * LANES)


def update_by_collectives(
    grads, square_weights, mlp_weights, gains, square_moment, mlp_moment, gain_moment, rate
):
    square_local, mlp_local, gain_local = from_wire(grads)
    square_grad, mlp_grad, gain_grad = (
        lax.psum_scatter(square_local, "dp", scatter_dimension=1, tiled=True),
        lax.psum_scatter(mlp_local, "dp", scatter_dimension=1, tiled=True),
        lax.psum_scatter(gain_local, "dp", scatter_dimension=1, tiled=True),
    )
    square_moment_new = 0.5 * square_moment + square_grad
    mlp_moment_new = 0.5 * mlp_moment + mlp_grad
    gain_moment_new = 0.5 * gain_moment + gain_grad
    device = lax.axis_index("dp")
    count = lax.axis_size("dp")
    square_owners = [index * count // 7 for index in range(5)]
    mlp_owners = [(index + 5) * count // 7 for index in range(2)]
    square_full, mlp_full = (
        lax.all_gather(square_moment_new, "dp", axis=1, tiled=True),
        lax.all_gather(mlp_moment_new, "dp", axis=1, tiled=True),
    )
    mine_square = pick_owned(square_full, square_owners, device)
    mine_mlp = pick_owned(mlp_full, mlp_owners, device)
    made_square = lax.cond(
        is_owner(square_owners, device), plain_orthogonalize, jnp.zeros_like, mine_square
    )
    made_mlp = lax.cond(is_owner(mlp_owners, device), plain_orthogonalize, jnp.zeros_like, mine_mlp)
    stack_square = jnp.stack(
        [jnp.where(device == owner, made_square, 0.0) for owner in square_owners]
    )
    stack_mlp = jnp.stack([jnp.where(device == owner, made_mlp, 0.0) for owner in mlp_owners])
    square_ortho, mlp_ortho = (
        lax.psum_scatter(stack_square, "dp", scatter_dimension=1, tiled=True),
        lax.psum_scatter(stack_mlp, "dp", scatter_dimension=1, tiled=True),
    )
    square_new = square_weights - jnp.array(SQ_RATES, F32)[:, None, None] * square_ortho
    mlp_new = mlp_weights - jnp.array(MLP_RATES, F32)[:, None, None] * mlp_ortho
    gains_new = gains - rate * gain_moment_new
    return (
        square_grad,
        square_moment_new,
        square_new,
        square_new.astype(BF16),
        mlp_grad,
        mlp_moment_new,
        mlp_new,
        mlp_new.astype(BF16),
        gain_grad,
        gain_moment_new,
        gains_new,
    )


def per_device(
    actions,
    observed,
    camera_flags,
    noise_levels,
    cotangent,
    square_weights,
    mlp_weights,
    gains,
    square_moment,
    mlp_moment,
    gain_moment,
):
    count = lax.axis_size("dp")
    rate = 0.1 / math.sqrt(actions.shape[0] * count)
    by_key = observed.transpose(1, 0, 2)
    ins = (actions, by_key, camera_flags, noise_levels, cotangent)
    if count == math.prod(GRID):
        made = block_and_back(True, *ins, square_weights, mlp_weights, gains, square_moment, mlp_moment)
        done = finish(rate, made, square_weights, mlp_weights, gains, gain_moment)
        output, actions_grad = done.output_f, done.ag_f
        d = done
        rest = (d.sqg, d.sqm, d.sqn, d.sqc, d.mlpg, d.mlpm, d.mlpn, d.mlpc, d.gg, d.gm, d.gn)
    else:
        square_all, mlp_all = (
            lax.all_gather(square_weights.astype(BF16), "dp", axis=1, tiled=True),
            lax.all_gather(mlp_weights.astype(BF16), "dp", axis=1, tiled=True),
        )
        gain_all = lax.all_gather(gains, "dp", axis=1, tiled=True)
        made = block_and_back(False, *ins, square_all, mlp_all, gain_all)
        done = finish(rate, made)
        output, actions_grad = made.output, made.ag
        grads = made.grads.reshape(-1, WIRE, LANES)
        rest = update_by_collectives(
            grads, square_weights, mlp_weights, gains, square_moment, mlp_moment, gain_moment, rate
        )
    observed_grad = done.og.transpose(1, 0, 2)
    return (output, actions_grad, observed_grad) + tuple(rest)


def solution(mesh):
    rows, cube, flat = P("dp", None), P("dp", None, None), P("dp")
    stacked, pair = P(None, "dp", None), P(None, "dp")
    return jax.shard_map(
        per_device,
        mesh=mesh,
        in_specs=(rows, cube, flat, flat, rows, stacked, stacked, pair, stacked, stacked, pair),
        out_specs=(rows, rows, cube) + (stacked,) * 8 + (pair,) * 3,
        check_vma=False,
    )
```

profile of v0, /device:TPU:0, one launch (start us, length us, event | category | flops | bytes accessed | tf_op | source)
XLA Modules:
  0.0 65.3 jit_solution(12072563596777593086)
XLA Ops:
  0.6 60.6 %block_and_back.1 = (f32[512,256]{1,0:T(8,128)S(1)}, f32[512,256]{1,0:T(8,128)S(1)}, bf16[196,32,256]{2,1,0:T(8,128)(2,1)S(1)}, f32[3,224,128]{2,1,0:T(8,128)S(1)}) custom-call(s32[32]{0:T(128)} %args_0_.4, s32[32]{0:T(128)} %args_1_.4, f32[512,256]{1,0:T(8,128)} %args_2_.4, bf16[196,32,256]{2,1,0:T(8,128)(2,1)} %bitcast.2, f32[512,256]{1,0:T(8,128)} %args_4_.5, ...), custom_call_target="tpu_custom_call" | custom-call | tf_op jit(solution)/shard_map/block_and_back/pallas_call | solution.py:976
  61.2 3.9 %finish.1 = (f32[196,32,256]{2,1,0:T(8,128)}, f32[512,256]{1,0:T(8,128)}, f32[512,256]{1,0:T(8,128)}, f32[5,8,256]{2,1,0:T(8,128)}, f32[5,8,256]{2,1,0:T(8,128)}...) custom-call(bf16[196,32,256]{2,1,0:T(8,128)(2,1)S(1)} %get-tuple-ele, ...), custom_call_target="tpu_custom_call" | custom-call | tf_op jit(solution)/shard_map/finish/pallas_call | solution.py:1096
where the time goes:
time: 65.5 us; the launch traced here: 65.3 us
  Pallas kernels  64.5 us (98%)
  between operations  0.82 us (1%)
    pallas_call x1, Pallas kernels, block_and_back(): pl.pallas_call(functools.partial(block_kernel, names, remote), out_shape=...  60.6 us
    pallas_call x1, Pallas kernels, finish(): pl.pallas_call(functools.partial(finish_kernel, names, rate), out_shape=t...  3.9 us

commit v1 on v0

--- a/solution.py
+++ b/solution.py
@@ -840,9 +840,9 @@
         update.two(7)
         update.three(6)
         turn_back(0, 0, chunks // 2)
+        update.three(7)
         update.orthogonalize()
         update.give_all()
-        update.three(7)
         turn_back(0, chunks // 2, chunks)
         update.four(4, 5, 6)
         turn_back(1, 0, chunks)

time: 65.5 us -> 64.6 us (0.986)
  Pallas kernels: 64.5 us -> 63.6 us
    pallas_call x1, Pallas kernels: 60.6 us -> 59.7 us  [block_and_back(): pl.pallas_call(functools.partial(block_kernel, names, remote), out_shape=...]
where the time goes in v1:
time: 64.6 us; the launch traced here: 64.4 us
  Pallas kernels  63.6 us (98%)
  between operations  0.82 us (1%)
    pallas_call x1, Pallas kernels, block_and_back(): pl.pallas_call(functools.partial(block_kernel, names, remote), out_shape=...  59.7 us
    pallas_call x1, Pallas kernels, finish(): pl.pallas_call(functools.partial(finish_kernel, names, rate), out_shape=t...  3.9 us

profile of v1, /device:TPU:0, one launch (start us, length us, event | category | flops | bytes accessed | tf_op | source)
XLA Modules:
  0.0 64.4 jit_solution(9952605121602353497)
XLA Ops:
  0.6 59.7 %block_and_back.1 = (f32[512,256]{1,0:T(8,128)S(1)}, f32[512,256]{1,0:T(8,128)S(1)}, bf16[196,32,256]{2,1,0:T(8,128)(2,1)S(1)}, f32[3,224,128]{2,1,0:T(8,128)S(1)}) custom-call(s32[32]{0:T(128)} %args_0_.4, s32[32]{0:T(128)} %args_1_.4, f32[512,256]{1,0:T(8,128)} %args_2_.4, bf16[196,32,256]{2,1,0:T(8,128)(2,1)} %bitcast.2, f32[512,256]{1,0:T(8,128)} %args_4_.5, ...), custom_call_target="tpu_custom_call" | custom-call | tf_op jit(solution)/shard_map/block_and_back/pallas_call | solution.py:976
  60.4 3.9 %finish.1 = (f32[196,32,256]{2,1,0:T(8,128)}, f32[512,256]{1,0:T(8,128)}, f32[512,256]{1,0:T(8,128)}, f32[5,8,256]{2,1,0:T(8,128)}, f32[5,8,256]{2,1,0:T(8,128)}...) custom-call(bf16[196,32,256]{2,1,0:T(8,128)(2,1)S(1)} %get-tuple-ele, ...), custom_call_target="tpu_custom_call" | custom-call | tf_op jit(solution)/shard_map/finish/pallas_call | solution.py:1096

commit v2 on v1

--- a/solution.py
+++ b/solution.py
@@ -167,7 +167,7 @@
             self.plane(k, False, True).wait_send()
             self.core(k, True).wait_send()
 
-    def fill(self):
+    def fill(self, square):
         r = self.r
         spot = (self.z, self.y, self.x, self.c)
 
@@ -176,10 +176,12 @@
                 pair = [source[m, :, pl.ds((2 * j + k) * LANES, LANES)] for k in range(2)]
                 r.wire[spot + (pl.ds(base + j * 16, 16),)] = jnp.concatenate(pair, axis=0).astype(BF16)
 
+        if not square:
+            for m in range(2):
+                tiles(r.mlpw_v, m, m * MLP_ROWS, 4)
+            return
         for m in range(5):
             tiles(r.sqw_v, m, SQ_AT[m], 1)
-        for m in range(2):
-            tiles(r.mlpw_v, m, m * MLP_ROWS, 4)
         gains, edge = r.gain_v[...], r.edge
         high = gains.astype(BF16).astype(F32)
         middle = (gains - high).astype(BF16).astype(F32)
@@ -520,10 +522,13 @@
     if remote:
         gather, update = Gather(r), Update(r)
         expected = greet_all()
-        arrive(0, 1, 2)
-        gather.fill()
+        arrive(0, 2)
+        gather.fill(True)
         pl.semaphore_wait(pltpu.get_barrier_semaphore(), expected)
-        gather.first(5, 6, 4, 0, 1, 2, 3)
+        gather.first(5, 6, 4)
+        arrive(1)
+        gather.fill(False)
+        gather.first(0, 1, 2, 3)
 
     arrive(3)
 
@@ -829,20 +834,21 @@
         update.start(7)
         update.one(6)
         update.three(4)
-        memory_back(0, pairs // 2)
+        memory_back(0, 6)
         update.four(2, 3)
         update.two(5)
         update.one(7)
         update.two(6)
-        memory_back(pairs // 2, pairs)
+        memory_back(6, 11)
         update.four(0, 1)
         update.three(5)
         update.two(7)
         update.three(6)
-        turn_back(0, 0, chunks // 2)
+        memory_back(11, pairs)
         update.three(7)
         update.orthogonalize()
         update.give_all()
+        turn_back(0, 0, chunks // 2)
         turn_back(0, chunks // 2, chunks)
         update.four(4, 5, 6)
         turn_back(1, 0, chunks)
@@ -985,7 +991,7 @@
     return Refs(zip(outs, results))
 
 
-PARTS = 7
+PARTS = 14
 
 
 def finish_kernel(names, rate, *args):

time: 64.6 us -> 64.5 us (level)
  no operation moved by 1% of the time
where the time goes in v2:
time: 64.5 us; the launch traced here: 64.4 us
  Pallas kernels  63.6 us (99%)
  between operations  0.82 us (1%)
    pallas_call x1, Pallas kernels, block_and_back(): pl.pallas_call(functools.partial(block_kernel, names, remote), out_shape=...  59.6 us
    pallas_call x1, Pallas kernels, finish(): pl.pallas_call(functools.partial(finish_kernel, names, rate), out_shape=t...  3.93 us

profile of v2, /device:TPU:0, one launch (start us, length us, event | category | flops | bytes accessed | tf_op | source)
XLA Modules:
  0.0 64.4 jit_solution(15889515064891117599)
XLA Ops:
  0.6 59.6 %block_and_back.1 = (f32[512,256]{1,0:T(8,128)S(1)}, f32[512,256]{1,0:T(8,128)S(1)}, bf16[196,32,256]{2,1,0:T(8,128)(2,1)S(1)}, f32[3,224,128]{2,1,0:T(8,128)S(1)}) custom-call(s32[32]{0:T(128)} %args_0_.4, s32[32]{0:T(128)} %args_1_.4, f32[512,256]{1,0:T(8,128)} %args_2_.4, bf16[196,32,256]{2,1,0:T(8,128)(2,1)} %bitcast.2, f32[512,256]{1,0:T(8,128)} %args_4_.5, ...), custom_call_target="tpu_custom_call" | custom-call | tf_op jit(solution)/shard_map/block_and_back/pallas_call | solution.py:982
  60.3 3.9 %finish.1 = (f32[196,32,256]{2,1,0:T(8,128)}, f32[512,256]{1,0:T(8,128)}, f32[512,256]{1,0:T(8,128)}, f32[5,8,256]{2,1,0:T(8,128)}, f32[5,8,256]{2,1,0:T(8,128)}...) custom-call(bf16[196,32,256]{2,1,0:T(8,128)(2,1)S(1)} %get-tuple-ele, ...), custom_call_target="tpu_custom_call" | custom-call | tf_op jit(solution)/shard_map/finish/pallas_call | solution.py:1102
